TPU v7x, 32 devices: a whole 2x2x4 slice. The times are simulated.
32 devices in a mesh: dp: 2 (over y), expert: 16 (over z, x, core).
Axes of the slice: x: 2, y: 2, z: 4, core: 2. Of those that a mesh axis runs over, the one named last changes fastest.
Arguments:
- cache: bfloat16 [4, 64, 1152], P('dp'), may hold values from -6 to 6
- requests: int32 [2, 16, 2], P(None, 'expert'), may hold values from 0 to 3
- routes: int32 [4096, 1], P('expert'), may hold values from 0 to 15; in each aligned block of 256 rows (0 to 255, 256 to 511, ...) at most 20 rows name the same one
- combine_weight: float32 [4096, 1], P('expert'), may hold values from 0.2 to 1
- proj_weight: bfloat16 [1152, 2048], P('expert', 'dp'), may hold values from -1 to 1
- norm_gain: float32 [2048], replicated, may hold values from 0.5 to 1.5
- gate_weight: bfloat16 [16, 2048, 1408], P('expert', None, 'dp'), may hold values from -0.125 to 0.125
- up_weight: bfloat16 [16, 2048, 1408], P('expert', None, 'dp'), may hold values from -0.125 to 0.125
- down_weight: bfloat16 [16, 1408, 2048], P('expert', None, 'dp'), may hold values from -0.15625 to 0.15625
- cotangent: bfloat16 [4096, 2048], P('expert', 'dp'), may hold values from -6 to 6
Outputs:
- mixed: bfloat16 [4096, 2048], P('expert', 'dp')
- down_grad: bfloat16 [16, 1408, 2048], P('expert', None, 'dp')
Inputs may be any that keep to these rules, and one draw needn't show every extreme that they name: `routes`: among the 256 tokens of one column no expert is named more than 20 times, and in every draw some column names some expert exactly 20 times.
All inputs are finite; a program needn't handle non-finite values.
Results may differ from a plain program's by a relative error of at most 0.012.
Values may be sent and summed in bfloat16 or wider, within the bound.
A program may use at most 64 MiB of HBM per device.

v0:
```python
import jax
import jax.numpy as jnp
from jax import lax
from jax.sharding import PartitionSpec as P


def normalize(row_block, gain_row, sum_squares, model_width):
    inv_scale = lax.rsqrt(sum_squares / model_width + 1e-06)
    return (row_block.astype(jnp.float32) * inv_scale[:, None] * gain_row[None, :]).astype(
        jnp.bfloat16
    )


def local_squares(row_block):
    values = row_block.astype(jnp.float32)
    return jnp.sum(values * values, axis=1)


def body(
    cache,
    requests,
    routes,
    combine_weight,
    proj_weight,
    norm_gain,
    gate_weight,
    up_weight,
    down_weight,
    cotangent,
):
    dp_rank = lax.axis_index("dp")
    model_width = norm_gain.shape[0]
    slice_width = cotangent.shape[1]
    wanted = requests.reshape(-1)
    request_count = wanted.shape[0]
    shard_piece = lax.all_gather(cache, "dp", axis=0, tiled=True)
    matches = (wanted[:, None] == jnp.arange(shard_piece.shape[0])[None, :]).astype(jnp.bfloat16)
    matched = jnp.einsum("rk,kpf->rpf", matches, shard_piece, preferred_element_type=jnp.float32)
    fetched = matched.astype(jnp.bfloat16)
    features = fetched.reshape(request_count * cache.shape[1], cache.shape[2])
    tokens = features.shape[0]
    projected = jnp.dot(
        features,
        lax.all_gather(proj_weight, "expert", axis=0, tiled=True),
        preferred_element_type=jnp.float32,
    ).astype(jnp.bfloat16)
    gain_slice = lax.dynamic_slice_in_dim(norm_gain, dp_rank * slice_width, slice_width)
    sum_squares = lax.psum(local_squares(projected), "dp")
    source_rows = normalize(projected, gain_slice, sum_squares, model_width)
    experts = lax.axis_size("expert") * gate_weight.shape[0]
    capacity = max(2, 5 * tokens // (4 * experts))
    expert_id = routes[:, 0]
    onehot = (expert_id[:, None] == jnp.arange(experts, dtype=jnp.int32)[None, :]).astype(jnp.int32)
    slot_rank = jnp.sum((jnp.cumsum(onehot, axis=0) - 1) * onehot, axis=1)
    position = expert_id * capacity + slot_rank
    slot_map = (
        jnp.zeros((experts * capacity,), jnp.int32)
        .at[position]
        .set(jnp.arange(tokens, dtype=jnp.int32) + 1)
    )
    filled = slot_map > 0
    source_row = jnp.maximum(slot_map - 1, 0)

    def arrange(row_block):
        picked = jnp.where(filled[:, None], row_block[source_row], jnp.zeros((), row_block.dtype))
        return picked.reshape(experts, capacity, row_block.shape[1])

    token_weight = combine_weight[:, 0]
    scaled_grad = (token_weight[:, None] * cotangent.astype(jnp.float32)).astype(jnp.bfloat16)
    sent_rows, sent_grad = (
        lax.all_to_all(arrange(source_rows), "expert", split_axis=0, concat_axis=0, tiled=True),
        lax.all_to_all(arrange(scaled_grad), "expert", split_axis=0, concat_axis=0, tiled=True),
    )
    slot_count = sent_rows.shape[0] * sent_rows.shape[1]
    full_rows = lax.all_gather(sent_rows.reshape(slot_count, slice_width), "dp", axis=1, tiled=True)
    grad_rows = sent_grad.reshape(slot_count, slice_width)
    gate_act = jnp.dot(full_rows, gate_weight[0], preferred_element_type=jnp.float32)
    up_act = jnp.dot(full_rows, up_weight[0], preferred_element_type=jnp.float32)
    hidden = (jax.nn.silu(gate_act) * up_act).astype(jnp.bfloat16)
    down_local = down_weight[0]
    shard_piece = lax.all_gather(hidden, "dp", axis=1, tiled=True)
    out_sum = jnp.dot(shard_piece, down_local, preferred_element_type=jnp.float32)
    grad_block = lax.dot_general(
        shard_piece, grad_rows, (((0,), (0,)), ((), ())), preferred_element_type=jnp.float32
    )
    grad_sum = grad_block
    out_sum, grad_sum = (out_sum, grad_sum)
    expert_out = out_sum.astype(jnp.bfloat16).reshape(sent_rows.shape[0], capacity, slice_width)
    returned = lax.all_to_all(expert_out, "expert", split_axis=0, concat_axis=0, tiled=True)
    returned_flat = returned.reshape(experts * capacity, slice_width)
    mixed_out = (token_weight[:, None] * returned_flat[position].astype(jnp.float32)).astype(
        jnp.bfloat16
    )
    return (mixed_out, grad_sum.astype(jnp.bfloat16)[None])


def solution(mesh):
    return jax.shard_map(
        body,
        mesh=mesh,
        in_specs=(
            P("dp", None, None),
            P(None, "expert", None),
            P("expert", None),
            P("expert", None),
            P("expert", "dp"),
            P(),
            P("expert", None, "dp"),
            P("expert", None, "dp"),
            P("expert", None, "dp"),
            P("expert", "dp"),
        ),
        out_specs=(P("expert", "dp"), P("expert", None, "dp")),
        check_vma=False,
    )
```

profile of v0, /device:TPU:9, one launch (start us, length us, event | category | flops | bytes accessed | tf_op | source)
XLA Modules:
  0.0 185.4 jit_solution(7512770705820136966)
XLA Ops:
  7.2 0.0 copy-start
  7.2 0.0 copy-start.1
  7.2 0.0 copy-start.2
  7.2 0.0 all-gather.4.cloned.1.call-start
  7.2 0.7 all-gather.4.cloned.1.call-update
  7.9 0.0 all-gather.6.cloned.1.call-start
  8.0 0.5 broadcast.80
  8.5 1.3 reduce.5
  9.8 0.1 eq.48
  9.9 8.8 %all_gather.12 = bf16[4,64,1152]{2,1,0:T(8,128)(2,1)S(1)} all-gather(bf16[2,64,1152]{2,1,0:T(8,128)(2,1)} %param.10), channel_id=1, replica_groups=mesh['dp'=2,'expert'=16] {'dp'}, dimensions={0}, use_global_device_ids=true | all-gather | bytes 884736 | tf_op jit(solution)/shard_map/all_gather | solution.py:36
  18.7 0.6 convolution_convert_fusion.1
  19.3 0.9 copy.19
  20.2 0.0 copy-done.1
  20.2 0.6 reduce-window.6
  20.8 0.2 slice_reduce_fusion
  21.0 0.1 fusion.24
  21.1 1.4 scatter_custom_fusion
  22.5 0.0 copy-done.2
  22.5 1.2 multiply_convert_fusion
  23.7 2.6 %gather_fusion.2 = bf16[320,1024]{1,0:T(8,128)(2,1)} fusion(bf16[256,1024]{1,0:T(8,128)(2,1)S(1)} %multiply_convert_fusion, s32[1024]{0:T(1024)S(1)} %pad_clamp_fusion.1), kind=kCustom, calls=%fused_computation.2 | custom fusion | bytes 1312000 | tf_op jit(solution)/shard_map/gather | solution.py:65
  26.4 2.0 %gather.17 = bf16[16,20,1024]{2,1,0:T(8,128)(2,1)} reshape(bf16[320,1024]{1,0:T(8,128)(2,1)} %gather_fusion.2) | data formatting | bytes 1310720 | tf_op jit(solution)/shard_map/gather | solution.py:65
  28.4 0.1 broadcast_in_dim.33
  28.5 0.0 dynamic-slice-start
  28.5 25.1 %all-gather.4.cloned.1.call-done = bf16[1152,1024]{1,0:T(8,128)(2,1)} async-done(((bf16[72,1024]{1,0:T(8,128)(2,1)}), bf16[1152,1024]{1,0:T(8,128)(2,1)}) %all-gather.4.cloned.1.call-update) | async-done | bytes 2359312 | tf_op jit(solution)/shard_map/all_gather | solution.py:44
  53.6 3.5 %fusion.19 = (f32[256]{0:T(256)S(1)}, bf16[256,1024]{1,0:T(8,128)(2,1)}) fusion(bf16[256,1152]{1,0:T(8,128)(2,1)} %bitcast.56, bf16[1152,1024]{1,0:T(8,128)(2,1)} %all-gather.4.cloned.1.call-done), kind=kOutput, calls=%fused_computation.20 | convolution fusion | flops 605028096 | bytes 3474432 | tf_op jit(solution)/shard_map/dot_general | solution.py:42
  57.1 3.8 %psum.7 = f32[256]{0:T(256)S(1)} all-reduce(f32[256]{0:T(256)S(1)} %get-tuple-element.4), channel_id=1, replica_groups=mesh['dp'=2,'expert'=16] {'dp'}, use_global_device_ids=true, to_apply=%region_5.6 | all-reduce | flops 256 | bytes 2048 | tf_op jit(solution)/shard_map/psum | solution.py:48
  60.9 0.0 dynamic-slice-done
  60.9 1.2 fusion.21
  62.1 2.6 %gather_fusion = bf16[320,1024]{1,0:T(8,128)(2,1)} fusion(bf16[256,1024]{1,0:T(8,128)(2,1)S(1)} %fusion.21, s32[1024]{0:T(1024)S(1)} %pad_clamp_fusion.1), kind=kCustom, calls=%fused_computation | custom fusion | bytes 1312000 | tf_op jit(solution)/shard_map/gather | solution.py:65
  64.8 2.0 %gather.14 = bf16[16,20,1024]{2,1,0:T(8,128)(2,1)} reshape(bf16[320,1024]{1,0:T(8,128)(2,1)} %gather_fusion) | data formatting | bytes 1310720 | tf_op jit(solution)/shard_map/gather | solution.py:65
  66.8 2.4 %broadcast_select_fusion = (bf16[16,20,1024]{2,1,0:T(8,128)(2,1)}, bf16[16,20,1024]{2,1,0:T(8,128)(2,1)S(1)}) fusion(bf16[16,20,1024]{2,1,0:T(8,128)(2,1)} %gather.17, pred[16,20]{1,0:T(8,128)(4,1)S(1)} %broadcast_in_dim.33, bf16[16,20,1024]{2,1,0:T(8,128)(2,1)} %gather.14), kind=kLoop, calls=%fused_computation.25 | loop fusion | flops 655360 | bytes 2621760 | tf_op jit(solution)/shard_map/jit(_where)/select_n | solution.py:65
  69.2 25.4 %all_to_all.15 = bf16[16,20,1024]{2,1,0:T(8,128)(2,1)} all-to-all(bf16[16,20,1024]{2,1,0:T(8,128)(2,1)S(1)} %get-tuple-element.3), channel_id=1, replica_groups=mesh['dp'=2,'expert'=16] {'expert'}, dimensions={0} | all-to-all | bytes 1310720 | tf_op jit(solution)/shard_map/all_to_all | solution.py:71
  94.6 2.0 %reshape.57 = bf16[320,1024]{1,0:T(8,128)(2,1)} reshape(bf16[16,20,1024]{2,1,0:T(8,128)(2,1)} %all_to_all.15) | data formatting | bytes 1310720 | tf_op jit(solution)/shard_map/reshape | solution.py:75
  96.6 0.0 all-gather.6.cloned.1.call-update
  96.6 4.5 %all-to-all-start.2 = ((bf16[16,20,1024]{2,1,0:T(8,128)(2,1)}), bf16[16,20,1024]{2,1,0:T(8,128)(2,1)}, u32[]{:S(2)}, u32[]{:S(2)}) async-start(bf16[16,20,1024]{2,1,0:T(8,128)(2,1)} %get-tuple-element.2), calls=%async_computation.2 | async-start | bytes 1572864 | tf_op jit(solution)/shard_map/all_to_all | solution.py:72
  101.1 18.7 %all-gather.6.cloned.1.call-done = bf16[320,2048]{1,0:T(8,128)(2,1)} async-done(((bf16[320,1024]{1,0:T(8,128)(2,1)}), bf16[320,2048]{1,0:T(8,128)(2,1)}) %all-gather.6.cloned.1.call-update) | async-done | bytes 1310736 | tf_op jit(solution)/shard_map/all_gather | solution.py:75
  119.8 0.0 copy-start.3
  119.8 0.0 copy-start.4
  119.8 3.6 %fusion.5 = f32[320,704]{1,0:T(8,128)S(1)} fusion(bf16[320,2048]{1,0:T(8,128)(2,1)} %all-gather.6.cloned.1.call-done, bf16[1,2048,704]{1,2,0:T(8,128)(2,1)} %param.16), kind=kOutput, calls=%fused_computation.10 | convolution fusion | flops 922746880 | bytes 5095424 | tf_op jit(solution)/shard_map/dot_general | solution.py:77
  123.4 0.0 copy-done.3
  123.4 0.0 copy-done.4
  123.4 1.3 fusion.16
  124.7 12.9 %all-gather = bf16[2,704,320]{1,2,0:T(8,128)(2,1)S(1)} all-gather(bf16[1,704,320]{1,2,0:T(8,128)(2,1)S(1)} %fusion.16), channel_id=1, replica_groups=mesh['dp'=2,'expert'=16] {'dp'}, dimensions={0}, use_global_device_ids=true | all-gather | bytes 1351680 | tf_op jit(solution)/shard_map/all_gather | solution.py:81
  137.6 2.0 %copy.20 = bf16[2,704,320]{1,0,2:T(2,128)(2,1)} copy(bf16[2,704,320]{1,2,0:T(8,128)(2,1)S(1)} %all-gather) | data formatting | bytes 1802240 | tf_op jit(solution)/shard_map/all_gather | solution.py:81
  139.6 3.4 %reshape.96 = bf16[1408,320]{0,1:T(8,128)(2,1)} reshape(bf16[2,704,320]{1,0,2:T(2,128)(2,1)} %copy.20) | data formatting | bytes 1802240
  143.0 0.0 copy-done
  143.0 2.4 %fusion.10 = bf16[320,1024]{1,0:T(8,128)(2,1)S(1)} fusion(bf16[1408,320]{0,1:T(8,128)(2,1)} %reshape.96, bf16[1,1408,1024]{2,1,0:T(8,128)(2,1)S(1)} %copy-done), kind=kOutput, calls=%fused_computation.14 | convolution fusion | flops 923074560 | bytes 4440064 | tf_op jit(solution)/shard_map/dot_general | solution.py:82
  145.4 1.0 reshape.58
  146.4 0.0 all-to-all-done.2
  146.4 7.2 %all-to-all-start.1 = ((bf16[16,20,1024]{2,1,0:T(8,128)(2,1)}), bf16[16,20,1024]{2,1,0:T(8,128)(2,1)}, u32[]{:S(2)}, u32[]{:S(2)}) async-start(bf16[16,20,1024]{2,1,0:T(8,128)(2,1)} %reshape.58), calls=%async_computation.1 | async-start | bytes 1572864 | tf_op jit(solution)/shard_map/all_to_all | solution.py:89
  153.7 1.3 reshape.60
  154.9 4.4 %fusion = bf16[1,1408,1024]{2,1,0:T(8,128)(2,1)} fusion(bf16[1408,320]{0,1:T(8,128)(2,1)} %reshape.96, bf16[320,1024]{1,0:T(8,128)(2,1)S(1)} %reshape.60), kind=kOutput, calls=%fused_computation.5 | convolution fusion | flops 924188672 | bytes 4440064 | tf_op jit(solution)/shard_map/dot_general | solution.py:83
  159.4 13.9 %all-to-all-done.1 = bf16[16,20,1024]{2,1,0:T(8,128)(2,1)} async-done(((bf16[16,20,1024]{2,1,0:T(8,128)(2,1)}), bf16[16,20,1024]{2,1,0:T(8,128)(2,1)}, u32[]{:S(2)}, u32[]{:S(2)}) %all-to-all-start.1) | async-done | bytes 655392 | tf_op jit(solution)/shard_map/all_to_all | solution.py:89
  173.3 1.2 reshape.59
  174.6 2.0 %gather_fusion.1 = bf16[256,1024]{1,0:T(8,128)(2,1)} fusion(bf16[320,1024]{1,0:T(8,128)(2,1)S(1)} %reshape.59, s32[1024]{0:T(1024)S(1)} %pad_clamp_fusion), kind=kCustom, calls=%fused_computation.1 | custom fusion | bytes 1049600 | tf_op jit(solution)/shard_map/gather | solution.py:91
  176.6 2.0 %multiply_convert_fusion.1 = bf16[256,1024]{1,0:T(8,128)(2,1)} fusion(bf16[256,1024]{1,0:T(8,128)(2,1)} %gather_fusion.1, f32[256]{0:T(256)S(1)} %bitcast.60), kind=kLoop, calls=%fused_computation.24 | loop fusion | flops 786432 | bytes 1049600 | tf_op jit(solution)/shard_map/convert_element_type | solution.py:91
  (10 shorter events, 0.1 us)
Async XLA Ops:
  7.2 135.9 %copy-start = (bf16[1,1408,1024]{2,1,0:T(8,128)(2,1)S(1)}, bf16[1,1408,1024]{2,1,0:T(8,128)(2,1)}, u32[]{:S(2)}) copy-start(bf16[1,1408,1024]{2,1,0:T(8,128)(2,1)} %param.18) | copy-start | bytes 8650756
  7.2 13.0 %copy-start.1 = (s32[256,1]{0,1:T(1,128)S(1)}, s32[256,1]{0,1:T(1,128)}, u32[]{:S(2)}) copy-start(s32[256,1]{0,1:T(1,128)} %param.12) | copy-start | bytes 3076
  7.2 15.3 %copy-start.2 = (f32[256,1]{0,1:T(1,128)S(1)}, f32[256,1]{0,1:T(1,128)}, u32[]{:S(2)}) copy-start(f32[256,1]{0,1:T(1,128)} %param.13) | copy-start | bytes 3076
  7.2 46.4 %all-gather.4.cloned.1.call-start = ((), (), s32[]{:S(2)}) async-start(), calls=%async_computation.3 | async-start | bytes 2506752 | tf_op jit(solution)/shard_map/all_gather | solution.py:44
  7.9 111.9 %all-gather.6.cloned.1.call-start = ((), (), s32[]{:S(2)}) async-start(), calls=%async_computation.4 | async-start | bytes 1966080 | tf_op jit(solution)/shard_map/all_gather | solution.py:75
  28.5 32.4 %dynamic-slice-start = ((f32[2048]{0:T(1024)}, s32[]{:T(128)}), f32[1024]{0:T(1024)S(1)}, s32[]{:S(2)}) async-start(f32[2048]{0:T(1024)} %param.15, s32[]{:T(128)} %select_n.20), calls=%async_computation.5 | async-start | bytes 8704 | tf_op jit(solution)/shard_map/dynamic_slice | solution.py:47
  96.6 49.8 %all-to-all-start.2 = ((bf16[16,20,1024]{2,1,0:T(8,128)(2,1)}), bf16[16,20,1024]{2,1,0:T(8,128)(2,1)}, u32[]{:S(2)}, u32[]{:S(2)}) async-start(bf16[16,20,1024]{2,1,0:T(8,128)(2,1)} %get-tuple-element.2), calls=%async_computation.2 | async-start | bytes 1572864 | tf_op jit(solution)/shard_map/all_to_all | solution.py:72
  119.8 3.6 %copy-start.3 = (bf16[1,2048,704]{1,2,0:T(8,128)(2,1)S(1)}, bf16[1,2048,704]{1,2,0:T(8,128)(2,1)}, u32[]{:S(2)}) copy-start(bf16[1,2048,704]{1,2,0:T(8,128)(2,1)} %param.17) | copy-start | bytes 8650756
  119.8 3.6 %copy-start.4 = (bf16[320,2048]{1,0:T(8,128)(2,1)S(1)}, bf16[320,2048]{1,0:T(8,128)(2,1)}, u32[]{:S(2)}) copy-start(bf16[320,2048]{1,0:T(8,128)(2,1)} %all-gather.6.cloned.1.call-done) | copy-start | bytes 3932164
  146.4 26.9 %all-to-all-start.1 = ((bf16[16,20,1024]{2,1,0:T(8,128)(2,1)}), bf16[16,20,1024]{2,1,0:T(8,128)(2,1)}, u32[]{:S(2)}, u32[]{:S(2)}) async-start(bf16[16,20,1024]{2,1,0:T(8,128)(2,1)} %reshape.58), calls=%async_computation.1 | async-start | bytes 1572864 | tf_op jit(solution)/shard_map/all_to_all | solution.py:89
Sparse Core Ops, SparseCore 0:
  10.3 43.2 all-gather.3
  96.7 23.0 all-gather.5
where the time goes:
time: 186 us; the launch traced here: 185 us
  waiting for transfers between devices  58.5 us (31%)
  blocking collectives  50.8 us (27%)
  local copies, waits for them, and re-layouts  25.4 us (14%)
  matrix products  15.8 us (8%)
  between operations  14.2 us (8%)
  starting transfers between devices  11.8 us (6%)
  other arithmetic  8.93 us (5%)
    all_to_all x1, blocking collectives, body(): lax.all_to_all(arrange(source_rows), 'expert', split_axis=0, concat_axis=...  25.4 us
    all_gather x1, waiting for transfers between devices, body(): lax.all_gather(proj_weight, 'expert', axis=0, tiled=True)  25.1 us
    all_gather x1, waiting for transfers between devices, body(): lax.all_gather(sent_rows.reshape(slot_count, slice_width), 'dp', axis=1,...  18.7 us
    all_to_all x1, waiting for transfers between devices, body(): lax.all_to_all(expert_out, 'expert', split_axis=0, concat_axis=0, tiled=T...  13.9 us
    all_gather x1, blocking collectives, body(): shard_piece = lax.all_gather(hidden, 'dp', axis=1, tiled=True)  12.9 us
    gather x4, local copies, waits for them, and re-layouts, arrange(): row_block[source_row]  9.29 us
    all_gather x1, blocking collectives, body(): shard_piece = lax.all_gather(cache, 'dp', axis=0, tiled=True)  8.75 us
    all_to_all x1, starting transfers between devices, body(): lax.all_to_all(expert_out, 'expert', split_axis=0, concat_axis=0, tiled=T...  7.25 us
  transfers between devices with their start and end apart: 4, of which 3 were waited for; matrix products, arithmetic and copies ran while one was open for 17% of the time, Pallas kernels for 0%

commit v1 on v0

--- a/solution.py
+++ b/solution.py
@@ -45,7 +45,7 @@
         preferred_element_type=jnp.float32,
     ).astype(jnp.bfloat16)
     gain_slice = lax.dynamic_slice_in_dim(norm_gain, dp_rank * slice_width, slice_width)
-    sum_squares = lax.psum(local_squares(projected), "dp")
+    sum_squares = jnp.sum(lax.all_gather(local_squares(projected), "dp"), axis=0)
     source_rows = normalize(projected, gain_slice, sum_squares, model_width)
     experts = lax.axis_size("expert") * gate_weight.shape[0]
     capacity = max(2, 5 * tokens // (4 * experts))

time: 186 us -> 186 us (level)
    psum x1 -> x0, blocking collectives: 3.77 us -> none  [body(): sum_squares = lax.psum(local_squares(projected), 'dp')]
    all_gather x0 -> x1, blocking collectives: none -> 3.08 us  [body(): lax.all_gather(local_squares(projected), 'dp')]
where the time goes in v1:
time: 186 us; the launch traced here: 185 us
  waiting for transfers between devices  58.5 us (31%)
  blocking collectives  50.1 us (27%)
  local copies, waits for them, and re-layouts  25.4 us (14%)
  matrix products  15.8 us (8%)
  between operations  14.2 us (8%)
  starting transfers between devices  11.8 us (6%)
  other arithmetic  8.95 us (5%)
    all_to_all x1, blocking collectives, body(): lax.all_to_all(arrange(source_rows), 'expert', split_axis=0, concat_axis=...  25.4 us
    all_gather x1, waiting for transfers between devices, body(): lax.all_gather(proj_weight, 'expert', axis=0, tiled=True)  25.1 us
    all_gather x1, waiting for transfers between devices, body(): lax.all_gather(sent_rows.reshape(slot_count, slice_width), 'dp', axis=1,...  18.7 us
    all_to_all x1, waiting for transfers between devices, body(): lax.all_to_all(expert_out, 'expert', split_axis=0, concat_axis=0, tiled=T...  13.9 us
    all_gather x1, blocking collectives, body(): shard_piece = lax.all_gather(hidden, 'dp', axis=1, tiled=True)  12.9 us
    gather x4, local copies, waits for them, and re-layouts, arrange(): row_block[source_row]  9.29 us
    all_gather x1, blocking collectives, body(): shard_piece = lax.all_gather(cache, 'dp', axis=0, tiled=True)  8.75 us
    all_to_all x1, starting transfers between devices, body(): lax.all_to_all(expert_out, 'expert', split_axis=0, concat_axis=0, tiled=T...  7.26 us
  transfers between devices with their start and end apart: 4, of which 3 were waited for; matrix products, arithmetic and copies ran while one was open for 17% of the time, Pallas kernels for 0%

profile of v1, /device:TPU:9, one launch (start us, length us, event | category | flops | bytes accessed | tf_op | source)
XLA Modules:
  0.0 184.7 jit_solution(11517015578774489140)
XLA Ops:
  7.2 0.0 copy-start
  7.2 0.0 copy-start.1
  7.2 0.0 copy-start.2
  7.2 0.0 all-gather.6.cloned.1.call-start
  7.2 0.7 all-gather.6.cloned.1.call-update
  7.9 0.0 all-gather.8.cloned.1.call-start
  8.0 0.5 broadcast.87
  8.5 1.3 reduce.6
  9.8 0.1 eq.48
  9.9 8.8 %all_gather.18 = bf16[4,64,1152]{2,1,0:T(8,128)(2,1)S(1)} all-gather(bf16[2,64,1152]{2,1,0:T(8,128)(2,1)} %param.10), channel_id=1, replica_groups=mesh['dp'=2,'expert'=16] {'dp'}, dimensions={0}, use_global_device_ids=true | all-gather | bytes 884736 | tf_op jit(solution)/shard_map/all_gather | solution.py:36
  18.7 0.6 convolution_convert_fusion.1
  19.3 0.9 copy.19
  20.2 0.0 copy-done.1
  20.2 0.6 reduce-window.6
  20.8 0.2 slice_reduce_fusion
  21.0 0.1 fusion.24
  21.1 1.4 scatter_custom_fusion
  22.5 0.0 copy-done.2
  22.5 1.2 multiply_convert_fusion
  23.7 2.6 %gather_fusion.2 = bf16[320,1024]{1,0:T(8,128)(2,1)} fusion(bf16[256,1024]{1,0:T(8,128)(2,1)S(1)} %multiply_convert_fusion, s32[1024]{0:T(1024)S(1)} %pad_clamp_fusion.1), kind=kCustom, calls=%fused_computation.2 | custom fusion | bytes 1312000 | tf_op jit(solution)/shard_map/gather | solution.py:65
  26.4 2.0 %gather.17 = bf16[16,20,1024]{2,1,0:T(8,128)(2,1)} reshape(bf16[320,1024]{1,0:T(8,128)(2,1)} %gather_fusion.2) | data formatting | bytes 1310720 | tf_op jit(solution)/shard_map/gather | solution.py:65
  28.4 0.1 broadcast_in_dim.33
  28.5 0.0 dynamic-slice-start
  28.5 25.1 %all-gather.6.cloned.1.call-done = bf16[1152,1024]{1,0:T(8,128)(2,1)} async-done(((bf16[72,1024]{1,0:T(8,128)(2,1)}), bf16[1152,1024]{1,0:T(8,128)(2,1)}) %all-gather.6.cloned.1.call-update) | async-done | bytes 2359312 | tf_op jit(solution)/shard_map/all_gather | solution.py:44
  53.6 3.5 %fusion.19 = (f32[256]{0:T(256)S(1)}, bf16[256,1024]{1,0:T(8,128)(2,1)}) fusion(bf16[256,1152]{1,0:T(8,128)(2,1)} %bitcast.57, bf16[1152,1024]{1,0:T(8,128)(2,1)} %all-gather.6.cloned.1.call-done), kind=kOutput, calls=%fused_computation.20 | convolution fusion | flops 605028096 | bytes 3474432 | tf_op jit(solution)/shard_map/dot_general | solution.py:42
  57.1 3.1 %all-gather.1 = f32[2,1,256]{2,1,0:T(1,128)S(1)} all-gather(f32[1,1,256]{2,1,0:T(1,128)S(1)} %bitcast.65), channel_id=2, replica_groups=mesh['dp'=2,'expert'=16] {'dp'}, dimensions={0}, use_global_device_ids=true | all-gather | bytes 3072 | tf_op jit(solution)/shard_map/all_gather | solution.py:48
  60.2 0.0 dynamic-slice-done
  60.2 1.2 fusion.21
  61.5 2.6 %gather_fusion = bf16[320,1024]{1,0:T(8,128)(2,1)} fusion(bf16[256,1024]{1,0:T(8,128)(2,1)S(1)} %fusion.21, s32[1024]{0:T(1024)S(1)} %pad_clamp_fusion.1), kind=kCustom, calls=%fused_computation | custom fusion | bytes 1312000 | tf_op jit(solution)/shard_map/gather | solution.py:65
  64.1 2.0 %gather.14 = bf16[16,20,1024]{2,1,0:T(8,128)(2,1)} reshape(bf16[320,1024]{1,0:T(8,128)(2,1)} %gather_fusion) | data formatting | bytes 1310720 | tf_op jit(solution)/shard_map/gather | solution.py:65
  66.1 2.4 %broadcast_select_fusion = (bf16[16,20,1024]{2,1,0:T(8,128)(2,1)}, bf16[16,20,1024]{2,1,0:T(8,128)(2,1)S(1)}) fusion(bf16[16,20,1024]{2,1,0:T(8,128)(2,1)} %gather.17, pred[16,20]{1,0:T(8,128)(4,1)S(1)} %broadcast_in_dim.33, bf16[16,20,1024]{2,1,0:T(8,128)(2,1)} %gather.14), kind=kLoop, calls=%fused_computation.25 | loop fusion | flops 655360 | bytes 2621760 | tf_op jit(solution)/shard_map/jit(_where)/select_n | solution.py:65
  68.5 25.4 %all_to_all.15 = bf16[16,20,1024]{2,1,0:T(8,128)(2,1)} all-to-all(bf16[16,20,1024]{2,1,0:T(8,128)(2,1)S(1)} %get-tuple-element.3), channel_id=1, replica_groups=mesh['dp'=2,'expert'=16] {'expert'}, dimensions={0} | all-to-all | bytes 1310720 | tf_op jit(solution)/shard_map/all_to_all | solution.py:71
  93.9 2.0 %reshape.61 = bf16[320,1024]{1,0:T(8,128)(2,1)} reshape(bf16[16,20,1024]{2,1,0:T(8,128)(2,1)} %all_to_all.15) | data formatting | bytes 1310720 | tf_op jit(solution)/shard_map/reshape | solution.py:75
  95.9 0.0 all-gather.8.cloned.1.call-update
  95.9 4.5 %all-to-all-start.2 = ((bf16[16,20,1024]{2,1,0:T(8,128)(2,1)}), bf16[16,20,1024]{2,1,0:T(8,128)(2,1)}, u32[]{:S(2)}, u32[]{:S(2)}) async-start(bf16[16,20,1024]{2,1,0:T(8,128)(2,1)} %get-tuple-element.2), calls=%async_computation.2 | async-start | bytes 1572864 | tf_op jit(solution)/shard_map/all_to_all | solution.py:72
  100.4 18.7 %all-gather.8.cloned.1.call-done = bf16[320,2048]{1,0:T(8,128)(2,1)} async-done(((bf16[320,1024]{1,0:T(8,128)(2,1)}), bf16[320,2048]{1,0:T(8,128)(2,1)}) %all-gather.8.cloned.1.call-update) | async-done | bytes 1310736 | tf_op jit(solution)/shard_map/all_gather | solution.py:75
  119.1 0.0 copy-start.3
  119.1 0.0 copy-start.4
  119.1 3.6 %fusion.5 = f32[320,704]{1,0:T(8,128)S(1)} fusion(bf16[320,2048]{1,0:T(8,128)(2,1)} %all-gather.8.cloned.1.call-done, bf16[1,2048,704]{1,2,0:T(8,128)(2,1)} %param.16), kind=kOutput, calls=%fused_computation.10 | convolution fusion | flops 922746880 | bytes 5095424 | tf_op jit(solution)/shard_map/dot_general | solution.py:77
  122.7 0.0 copy-done.3
  122.7 0.0 copy-done.4
  122.7 1.3 fusion.16
  124.0 12.9 %all-gather.2 = bf16[2,704,320]{1,2,0:T(8,128)(2,1)S(1)} all-gather(bf16[1,704,320]{1,2,0:T(8,128)(2,1)S(1)} %fusion.16), channel_id=1, replica_groups=mesh['dp'=2,'expert'=16] {'dp'}, dimensions={0}, use_global_device_ids=true | all-gather | bytes 1351680 | tf_op jit(solution)/shard_map/all_gather | solution.py:81
  137.0 2.0 %copy.20 = bf16[2,704,320]{1,0,2:T(2,128)(2,1)} copy(bf16[2,704,320]{1,2,0:T(8,128)(2,1)S(1)} %all-gather.2) | data formatting | bytes 1802240 | tf_op jit(solution)/shard_map/all_gather | solution.py:81
  138.9 3.4 %reshape.103 = bf16[1408,320]{0,1:T(8,128)(2,1)} reshape(bf16[2,704,320]{1,0,2:T(2,128)(2,1)} %copy.20) | data formatting | bytes 1802240
  142.4 0.0 copy-done
  142.4 2.4 %fusion.10 = bf16[320,1024]{1,0:T(8,128)(2,1)S(1)} fusion(bf16[1408,320]{0,1:T(8,128)(2,1)} %reshape.103, bf16[1,1408,1024]{2,1,0:T(8,128)(2,1)S(1)} %copy-done), kind=kOutput, calls=%fused_computation.14 | convolution fusion | flops 923074560 | bytes 4440064 | tf_op jit(solution)/shard_map/dot_general | solution.py:82
  144.7 1.0 reshape.62
  145.7 0.0 all-to-all-done.2
  145.8 7.3 %all-to-all-start.1 = ((bf16[16,20,1024]{2,1,0:T(8,128)(2,1)}), bf16[16,20,1024]{2,1,0:T(8,128)(2,1)}, u32[]{:S(2)}, u32[]{:S(2)}) async-start(bf16[16,20,1024]{2,1,0:T(8,128)(2,1)} %reshape.62), calls=%async_computation.1 | async-start | bytes 1572864 | tf_op jit(solution)/shard_map/all_to_all | solution.py:89
  153.0 1.3 reshape.64
  154.3 4.4 %fusion = bf16[1,1408,1024]{2,1,0:T(8,128)(2,1)} fusion(bf16[1408,320]{0,1:T(8,128)(2,1)} %reshape.103, bf16[320,1024]{1,0:T(8,128)(2,1)S(1)} %reshape.64), kind=kOutput, calls=%fused_computation.5 | convolution fusion | flops 924188672 | bytes 4440064 | tf_op jit(solution)/shard_map/dot_general | solution.py:83
  158.7 13.9 %all-to-all-done.1 = bf16[16,20,1024]{2,1,0:T(8,128)(2,1)} async-done(((bf16[16,20,1024]{2,1,0:T(8,128)(2,1)}), bf16[16,20,1024]{2,1,0:T(8,128)(2,1)}, u32[]{:S(2)}, u32[]{:S(2)}) %all-to-all-start.1) | async-done | bytes 655392 | tf_op jit(solution)/shard_map/all_to_all | solution.py:89
  172.7 1.2 reshape.63
  173.9 2.0 %gather_fusion.1 = bf16[256,1024]{1,0:T(8,128)(2,1)} fusion(bf16[320,1024]{1,0:T(8,128)(2,1)S(1)} %reshape.63, s32[1024]{0:T(1024)S(1)} %pad_clamp_fusion), kind=kCustom, calls=%fused_computation.1 | custom fusion | bytes 1049600 | tf_op jit(solution)/shard_map/gather | solution.py:91
  175.9 2.0 %multiply_convert_fusion.1 = bf16[256,1024]{1,0:T(8,128)(2,1)} fusion(bf16[256,1024]{1,0:T(8,128)(2,1)} %gather_fusion.1, f32[256]{0:T(256)S(1)} %bitcast.61), kind=kLoop, calls=%fused_computation.24 | loop fusion | flops 786432 | bytes 1049600 | tf_op jit(solution)/shard_map/convert_element_type | solution.py:91
  (11 shorter events, 0.1 us)
Async XLA Ops:
  7.2 135.2 %copy-start = (bf16[1,1408,1024]{2,1,0:T(8,128)(2,1)S(1)}, bf16[1,1408,1024]{2,1,0:T(8,128)(2,1)}, u32[]{:S(2)}) copy-start(bf16[1,1408,1024]{2,1,0:T(8,128)(2,1)} %param.18) | copy-start | bytes 8650756
  7.2 13.0 %copy-start.1 = (s32[256,1]{0,1:T(1,128)S(1)}, s32[256,1]{0,1:T(1,128)}, u32[]{:S(2)}) copy-start(s32[256,1]{0,1:T(1,128)} %param.12) | copy-start | bytes 3076
  7.2 15.3 %copy-start.2 = (f32[256,1]{0,1:T(1,128)S(1)}, f32[256,1]{0,1:T(1,128)}, u32[]{:S(2)}) copy-start(f32[256,1]{0,1:T(1,128)} %param.13) | copy-start | bytes 3076
  7.2 46.4 %all-gather.6.cloned.1.call-start = ((), (), s32[]{:S(2)}) async-start(), calls=%async_computation.3 | async-start | bytes 2506752 | tf_op jit(solution)/shard_map/all_gather | solution.py:44
  7.9 111.2 %all-gather.8.cloned.1.call-start = ((), (), s32[]{:S(2)}) async-start(), calls=%async_computation.4 | async-start | bytes 1966080 | tf_op jit(solution)/shard_map/all_gather | solution.py:75
  28.5 31.8 %dynamic-slice-start = ((f32[2048]{0:T(1024)}, s32[]{:T(128)}), f32[1024]{0:T(1024)S(1)}, s32[]{:S(2)}) async-start(f32[2048]{0:T(1024)} %param.15, s32[]{:T(128)} %select_n.20), calls=%async_computation.5 | async-start | bytes 8704 | tf_op jit(solution)/shard_map/dynamic_slice | solution.py:47
  95.9 49.8 %all-to-all-start.2 = ((bf16[16,20,1024]{2,1,0:T(8,128)(2,1)}), bf16[16,20,1024]{2,1,0:T(8,128)(2,1)}, u32[]{:S(2)}, u32[]{:S(2)}) async-start(bf16[16,20,1024]{2,1,0:T(8,128)(2,1)} %get-tuple-element.2), calls=%async_computation.2 | async-start | bytes 1572864 | tf_op jit(solution)/shard_map/all_to_all | solution.py:72
  119.1 3.6 %copy-start.3 = (bf16[1,2048,704]{1,2,0:T(8,128)(2,1)S(1)}, bf16[1,2048,704]{1,2,0:T(8,128)(2,1)}, u32[]{:S(2)}) copy-start(bf16[1,2048,704]{1,2,0:T(8,128)(2,1)} %param.17) | copy-start | bytes 8650756
  119.1 3.6 %copy-start.4 = (bf16[320,2048]{1,0:T(8,128)(2,1)S(1)}, bf16[320,2048]{1,0:T(8,128)(2,1)}, u32[]{:S(2)}) copy-start(bf16[320,2048]{1,0:T(8,128)(2,1)} %all-gather.8.cloned.1.call-done) | copy-start | bytes 3932164
  145.8 26.9 %all-to-all-start.1 = ((bf16[16,20,1024]{2,1,0:T(8,128)(2,1)}), bf16[16,20,1024]{2,1,0:T(8,128)(2,1)}, u32[]{:S(2)}, u32[]{:S(2)}) async-start(bf16[16,20,1024]{2,1,0:T(8,128)(2,1)} %reshape.62), calls=%async_computation.1 | async-start | bytes 1572864 | tf_op jit(solution)/shard_map/all_to_all | solution.py:89
Sparse Core Ops, SparseCore 0:
  10.3 43.2 all-gather.5
  96.0 23.0 all-gather.7
